TPU v7x, 32 devices: a whole 2x2x4 slice. The times are simulated.
32 devices in a mesh: blk: 16 (over z, x, core), grp: 2 (over y).
Axes of the slice: x: 2, y: 2, z: 4, core: 2. Of those that a mesh axis runs over, the one named last changes fastest.
Arguments:
- activations: bfloat16 [8192, 8192], P('blk', 'grp'), may hold values from -6 to 6
- output_grads: bfloat16 [8192, 28672], P('blk', 'grp'), may hold values from -6 to 6
- query_left: bfloat16 [32, 32, 8192], P('blk', None, 'grp'), may hold values from -0.0078125 to 0.0078125
- query_right: bfloat16 [32, 32, 28672], P('blk', None, 'grp'), may hold values from -0.00390625 to 0.00390625
- basis_inputs: bfloat16 [16, 8192, 256], P('blk', 'grp'), may hold values from -0.0625 to 0.0625
- eigen_inputs: bfloat16 [16, 256], P('blk'), may hold values from 0.099609375 to 100
- basis_outputs: bfloat16 [16, 28672, 512], P('blk', 'grp'), may hold values from -0.03125 to 0.03125
- eigen_outputs: bfloat16 [16, 512], P('blk'), may hold values from 0.099609375 to 100
- owners: int32 [2], replicated, may hold values from 0 to 15
- seq_lengths: int32 [64], P('blk'), may hold values from 1 to 128, as said below
Outputs:
- scores: float32 [64, 32], P('blk')
Inputs may be any that keep to these rules, and one draw needn't show every extreme that they name: `seq_lengths`: the 4 lengths of one shard sum to at most 512; in every draw some shard is full (all its lengths 128) and some sequence has length 1.
All inputs are finite; a program needn't handle non-finite values.
Results may differ from a plain program's by a relative error of at most 0.02.
Values may be sent and summed in bfloat16 or wider, within the bound.
A program may use at most 128 MiB of HBM per device.

v0:
```python
import jax
import jax.numpy as jnp
from jax import lax
from jax.sharding import PartitionSpec as P


def broadcast(x, axis, root):
    mine = lax.axis_index(axis) == root
    return lax.psum(jnp.where(mine, x, jnp.zeros_like(x)), axis)


def contract(row_block, factors):
    return lax.dot_general(
        row_block, factors, (((1,), (1,)), ((), ())), preferred_element_type=jnp.float32
    )


def finish(flat_rows, coeffs, basis, eigen):
    eigen_float = eigen.astype(jnp.float32)
    damped = (coeffs * (eigen_float / (1.0 + eigen_float))).astype(jnp.bfloat16)
    return (flat_rows.astype(jnp.float32) - contract(damped, basis)).astype(jnp.bfloat16)


def membership(seq_lens, slot_count):
    seq_ends = jnp.cumsum(seq_lens)
    seq_starts = seq_ends - seq_lens
    position = jnp.arange(slot_count, dtype=jnp.int32)[None, :]
    inside = (position >= seq_starts[:, None]) & (position < seq_ends[:, None])
    return inside.astype(jnp.float32)


def pair_scores(sum_left, sum_right, query_rank):
    product = (sum_left * sum_right).reshape(sum_left.shape[0], -1, query_rank)
    return jnp.sum(product, axis=2)


def local(
    activations,
    output_grads,
    query_left,
    query_right,
    basis_inputs,
    eigen_inputs,
    basis_outputs,
    eigen_outputs,
    owners,
    seq_lengths,
):
    basis_left, eigen_left = (
        broadcast(basis_inputs[0], "blk", owners[0]),
        broadcast(eigen_inputs[0], "blk", owners[0]),
    )
    basis_right, eigen_right = (
        broadcast(basis_outputs[0], "blk", owners[1]),
        broadcast(eigen_outputs[0], "blk", owners[1]),
    )
    query_rank = query_left.shape[1]
    left_flat = query_left.reshape(-1, query_left.shape[2])
    right_flat = query_right.reshape(-1, query_right.shape[2])
    left_coeffs = jnp.dot(left_flat, basis_left, preferred_element_type=jnp.float32)
    right_coeffs = jnp.dot(right_flat, basis_right, preferred_element_type=jnp.float32)
    left_coeffs, right_coeffs = (
        lax.psum(left_coeffs.astype(jnp.bfloat16), "grp").astype(jnp.float32),
        lax.psum(right_coeffs.astype(jnp.bfloat16), "grp").astype(jnp.float32),
    )
    left_ready = finish(left_flat, left_coeffs, basis_left, eigen_left).reshape(query_left.shape)
    right_ready = finish(right_flat, right_coeffs, basis_right, eigen_right).reshape(
        query_right.shape
    )
    slot_count = activations.shape[0]
    pieces = (
        lax.all_gather(left_ready, "blk", axis=0, tiled=True),
        lax.all_gather(right_ready, "blk", axis=0, tiled=True),
    )
    left_piece = pieces[0].reshape(-1, pieces[0].shape[2])
    right_piece = pieces[1].reshape(-1, pieces[1].shape[2])
    new_left = contract(activations, left_piece)
    new_right = contract(output_grads, right_piece)
    member = membership(seq_lengths, slot_count)
    share_left, share_right = (
        lax.psum_scatter(
            new_left.astype(jnp.bfloat16), "grp", scatter_dimension=0, tiled=True
        ).astype(jnp.float32),
        lax.psum_scatter(
            new_right.astype(jnp.bfloat16), "grp", scatter_dimension=0, tiled=True
        ).astype(jnp.float32),
    )
    share_rows = share_left.shape[0]
    member_part = lax.dynamic_slice_in_dim(
        member, lax.axis_index("grp") * share_rows, share_rows, 1
    )
    partial_scores = jnp.dot(
        member_part,
        pair_scores(share_left, share_right, query_rank),
        precision=lax.Precision.HIGHEST,
        preferred_element_type=jnp.float32,
    )
    result = lax.psum(partial_scores, "grp")
    return result


def solution(mesh):
    in_specs = (
        P("blk", "grp"),
        P("blk", "grp"),
        P("blk", None, "grp"),
        P("blk", None, "grp"),
        P("blk", "grp", None),
        P("blk", None),
        P("blk", "grp", None),
        P("blk", None),
        P(),
        P("blk"),
    )
    out_specs = P("blk", None)
    return jax.shard_map(local, mesh=mesh, in_specs=in_specs, out_specs=out_specs, check_vma=False)
```

profile of v0, /device:TPU:0, one launch (start us, length us, event | category | flops | bytes accessed | tf_op | source)
XLA Modules:
  0.0 651.4 jit_solution(9754801800257341346)
XLA Ops:
  6.5 1.4 fusion.19
  9.3 5.9 select_bitcast_fusion
  15.2 1.5 select_bitcast_fusion.1
  16.6 0.0 all-reduce.5.cloned.1.call-start
  16.7 0.6 copy-done.4
  17.3 36.2 %all-reduce = (bf16[512]{0:T(512)(128)(2,1)S(1)}, bf16[256]{0:T(256)(128)(2,1)S(1)}) all-reduce(bf16[512]{0:T(512)(128)(2,1)S(1)} %fusion.14, bf16[256]{0:T(256)(128)(2,1)S(1)} %fusion.18), channel_id=1, replica_groups=mesh['blk'=16,'grp'=2] {'blk'}, use_global_device_ids=true, to_apply=%region_7.8 | all-reduce | flops 768 | bytes 3072 | tf_op jit(solution)/shard_map/psum | solution.py:9
  53.5 271.7 %all-reduce.7.cloned.1.call-done = (bf16[14336,512]{1,0:T(8,128)(2,1)}, bf16[4096,256]{1,0:T(8,128)(2,1)}) async-done(((bf16[14336,512]{1,0:T(8,128)(2,1)}, bf16[4096,256]{1,0:T(8,128)(2,1)}), (bf16[14336,512]{1,0:T(8,128)(2,1)}, bf16[4096,256]{1,0:T(8,128)(2,1)})) %all-reduce.7.cloned.1.call-update) | async-done | bytes 16777232 | tf_op jit(solution)/shard_map/psum | solution.py:9
  325.2 2.3 fusion.5
  327.6 8.8 %psum.50 = bf16[64,256]{0,1:T(8,128)(2,1)S(1)} all-reduce(bf16[64,256]{0,1:T(8,128)(2,1)S(1)} %fusion.5), channel_id=1, replica_groups=mesh['blk'=16,'grp'=2] {'grp'}, use_global_device_ids=true, to_apply=%region_2.3 | all-reduce | flops 16384 | bytes 65536 | tf_op jit(solution)/shard_map/psum | solution.py:63
  336.4 10.5 %fusion.4 = bf16[64,512]{0,1:T(8,128)(2,1)} fusion(bf16[14336,512]{1,0:T(8,128)(2,1)} %get-tuple-element.7, bf16[64,14336]{1,0:T(8,128)(2,1)} %bitcast.38), kind=kOutput, calls=%fused_computation.11 | convolution fusion | flops 939556864 | bytes 16580608 | tf_op jit(solution)/shard_map/dot_general | solution.py:61
  347.0 1.6 fusion.1
  348.7 18.6 %all-reduce.5.cloned.1.call-done = bf16[64,512]{0,1:T(8,128)(2,1)} async-done(((bf16[64,512]{0,1:T(8,128)(2,1)}), bf16[64,512]{0,1:T(8,128)(2,1)}) %all-reduce.5.cloned.1.call-update) | async-done | bytes 65552 | tf_op jit(solution)/shard_map/psum | solution.py:64
  367.3 11.6 %fusion = bf16[64,14336]{1,0:T(8,128)(2,1)} fusion(bf16[14336,512]{1,0:T(8,128)(2,1)} %get-tuple-element.7, bf16[64,14336]{1,0:T(8,128)(2,1)} %bitcast.39, bf16[64,512]{0,1:T(8,128)(2,1)} %all-reduce.5.cloned.1.call-done, f32[512]{0:T(512)S(1)} %add_divide_fusion), kind=kOutput, calls=%fused_computation.1 | convolution fusion | flops 942374912 | bytes 18417664 | tf_op jit(solution)/shard_map/dot_general | solution.py:13
  379.0 0.2 reduce-scatter.3.cloned.1.call-start
  379.2 65.2 %all-gather.3.cloned.1.call-done = bf16[32,32,4096]{2,1,0:T(8,128)(2,1)} async-done(((bf16[2,32,4096]{2,1,0:T(8,128)(2,1)}), bf16[32,32,4096]{2,1,0:T(8,128)(2,1)}) %all-gather.3.cloned.1.call-update) | async-done | bytes 8388624 | tf_op jit(solution)/shard_map/all_gather | solution.py:72
  444.4 10.1 %fusion.2 = bf16[512,1024]{0,1:T(8,128)(2,1)} fusion(bf16[1024,4096]{1,0:T(8,128)(2,1)} %bitcast.43, bf16[512,4096]{1,0:T(8,128)(2,1)} %param.10), kind=kOutput, calls=%fused_computation.8 | convolution fusion | flops 4295491584 | bytes 13631488 | tf_op jit(solution)/shard_map/dot_general | solution.py:13
  454.5 0.0 reduce-scatter.5.cloned.1.call-start
  454.6 137.9 %all-gather.5.cloned.1.call-done = bf16[32,32,14336]{2,1,0:T(8,128)(2,1)} async-done(((bf16[2,32,14336]{2,1,0:T(8,128)(2,1)}), bf16[32,32,14336]{2,1,0:T(8,128)(2,1)}) %all-gather.5.cloned.1.call-update) | async-done | bytes 29360144 | tf_op jit(solution)/shard_map/all_gather | solution.py:73
  592.5 22.8 %fusion.3 = bf16[512,1024]{0,1:T(8,128)(2,1)} fusion(bf16[1024,14336]{1,0:T(8,128)(2,1)} %bitcast.42, bf16[512,14336]{1,0:T(8,128)(2,1)} %param.11), kind=kOutput, calls=%fused_computation.9 | convolution fusion | flops 15032909824 | bytes 45088768 | tf_op jit(solution)/shard_map/dot_general | solution.py:13
  615.3 0.2 reduce-window.8
  615.5 22.0 %reduce-scatter.5.cloned.1.call-done = bf16[256,1024]{0,1:T(8,128)(2,1)} async-done(((bf16[512,1024]{0,1:T(8,128)(2,1)}), bf16[256,1024]{0,1:T(8,128)(2,1)}) %reduce-scatter.5.cloned.1.call-update) | async-done | bytes 524304 | tf_op jit(solution)/shard_map/reduce_scatter | solution.py:84
  637.5 1.4 bitcast_reduce_fusion
  638.9 0.2 fusion.11
  639.1 5.5 psum.55
  (26 shorter events, 0.3 us)
Async XLA Ops:
  6.5 318.7 %all-reduce.7.cloned.1.call-start = ((), (), s32[]{:S(2)}) async-start(), calls=%async_computation.7 | async-start | bytes 33554432 | tf_op jit(solution)/shard_map/psum | solution.py:9
  9.3 5.9 copy-start
  16.6 0.7 copy-start.4
  16.6 0.7 copy-start.3
  16.6 308.6 %copy-start.2 = (bf16[2,32,4096]{2,1,0:T(8,128)(2,1)S(1)}, bf16[2,32,4096]{2,1,0:T(8,128)(2,1)}, u32[]{:S(2)}) copy-start(bf16[2,32,4096]{2,1,0:T(8,128)(2,1)} %param.12) | copy-start | bytes 1572868
  16.6 350.7 %all-reduce.5.cloned.1.call-start = ((), (), s32[]{:S(2)}) async-start(), calls=%async_computation.4 | async-start | bytes 262144 | tf_op jit(solution)/shard_map/psum | solution.py:64
  336.4 10.6 %copy-start.1 = (bf16[4096,256]{1,0:T(8,128)(2,1)S(1)}, bf16[4096,256]{1,0:T(8,128)(2,1)}, u32[]{:S(2)}) copy-start(bf16[4096,256]{1,0:T(8,128)(2,1)} %get-tuple-element.8) | copy-start | bytes 6291460
  346.9 97.5 %all-gather.3.cloned.1.call-start = ((), (), s32[]{:S(2)}) async-start(), calls=%async_computation.2 | async-start | bytes 8912896 | tf_op jit(solution)/shard_map/all_gather | solution.py:72
  348.6 243.9 %all-gather.5.cloned.1.call-start = ((), (), s32[]{:S(2)}) async-start(), calls=%async_computation.5 | async-start | bytes 31195136 | tf_op jit(solution)/shard_map/all_gather | solution.py:73
  379.0 236.5 %reduce-scatter.3.cloned.1.call-start = ((), (), s32[]{:S(2)}) async-start(), calls=%async_computation.3 | async-start | bytes 1572864 | tf_op jit(solution)/shard_map/reduce_scatter | solution.py:81
  454.5 182.9 %reduce-scatter.5.cloned.1.call-start = ((), (), s32[]{:S(2)}) async-start(), calls=%async_computation.6 | async-start | bytes 1572864 | tf_op jit(solution)/shard_map/reduce_scatter | solution.py:84
  592.5 22.8 %copy-start.5 = (s32[4]{0:T(128)S(1)}, s32[4]{0:T(128)}, u32[]{:S(2)}) copy-start(s32[4]{0:T(128)} %param.19) | copy-start | bytes 52
Sparse Core Ops, SparseCore 0:
  16.8 308.4 all-reduce.6
  347.0 20.2 all-reduce.4
  369.5 74.8 all-gather.2
  445.9 146.5 all-gather.4
  594.6 20.2 reduce-scatter.2
  617.1 20.3 reduce-scatter.4
where the time goes:
time: 651 us
  waiting for transfers between devices  516 us (79%)
  matrix products  59.1 us (9%)
  blocking collectives  50.5 us (8%)
  between operations  14.9 us (2%)
  other arithmetic  9.01 us (1%)
    psum x1, waiting for transfers between devices, broadcast(): return lax.psum(jnp.where(mine, x, jnp.zeros_like(x)), axis)  272 us
    all_gather x1, waiting for transfers between devices, local(): lax.all_gather(right_ready, 'blk', axis=0, tiled=True)  138 us
    all_gather x1, waiting for transfers between devices, local(): lax.all_gather(left_ready, 'blk', axis=0, tiled=True)  65.2 us
    dot_general x4, matrix products, contract(): lax.dot_general(row_block, factors, (((1,), (1,)), ((), ())), preferred_e...  46.1 us
    psum x1, blocking collectives, broadcast(): return lax.psum(jnp.where(mine, x, jnp.zeros_like(x)), axis)  36.2 us
    reduce_scatter x1, waiting for transfers between devices, local(): lax.psum_scatter(new_right.astype(jnp.bfloat16), 'grp', scatter_dimension...  22 us
    psum x1, waiting for transfers between devices, local(): lax.psum(right_coeffs.astype(jnp.bfloat16), 'grp').astype(jnp.float32)  18.6 us
  transfers between devices with their start and end apart: 6, of which 5 were waited for; matrix products, arithmetic and copies ran while one was open for 7% of the time, Pallas kernels for 0%

commit v1 on v0

v1 whole, which is shorter than its diff:
```python
import functools

import jax
import jax.numpy as jnp
from jax import lax
from jax.experimental import pallas as pl
from jax.experimental.pallas import tpu as pltpu
from jax.sharding import PartitionSpec as P

MESH = pl.DeviceIdType.MESH
HBM = pl.BlockSpec(memory_space=pltpu.HBM)


def broadcast(x, axis, root):
    mine = lax.axis_index(axis) == root
    return lax.psum(jnp.where(mine, x, jnp.zeros_like(x)), axis)


def contract(row_block, factors):
    return lax.dot_general(
        row_block, factors, (((1,), (1,)), ((), ())), preferred_element_type=jnp.float32
    )


def finish(flat_rows, coeffs, basis, eigen):
    eigen_float = eigen.astype(jnp.float32)
    damped = (coeffs * (eigen_float / (1.0 + eigen_float))).astype(jnp.bfloat16)
    return (flat_rows.astype(jnp.float32) - contract(damped, basis)).astype(jnp.bfloat16)


def membership(seq_lens, slot_count):
    seq_ends = jnp.cumsum(seq_lens)
    seq_starts = seq_ends - seq_lens
    position = jnp.arange(slot_count, dtype=jnp.int32)[None, :]
    inside = (position >= seq_starts[:, None]) & (position < seq_ends[:, None])
    return inside.astype(jnp.float32)


def grid_of(chips):
    cols = 1
    while cols * cols * 4 <= chips:
        cols *= 2
    return chips // cols, cols


def chip_at(place, chips):
    rows, cols = grid_of(chips)
    if cols == 1:
        return place
    wide = cols - 1
    row, step = place // wide, place % wide
    col = jnp.where(row % 2 == 0, 1 + step, wide - step)
    back = chips - 1 - place
    return jnp.where(place < rows * wide, row * cols + col, back * cols)


def place_of(chip, chips):
    rows, cols = grid_of(chips)
    if cols == 1:
        return chip
    wide = cols - 1
    row, col = chip // cols, chip % cols
    step = jnp.where(row % 2 == 0, col - 1, wide - col)
    return jnp.where(col == 0, chips - 1 - row, row * wide + step)


def wide_tile(width):
    tile = 2048
    while width % tile:
        tile //= 2
    return tile


def gather_kernel(
    chips,
    rows,
    act_ref,
    grad_ref,
    left_ref,
    right_ref,
    proj_left,
    proj_right,
    all_left,
    all_right,
    act,
    grad,
    block_left,
    block_right,
    total,
    load_sem,
    own_sem,
    ring_send,
    ring_recv,
    twin_send,
    twin_recv,
):
    me = lax.axis_index("blk")
    chip, core = me // 2, me % 2
    place = place_of(chip, chips)
    after = chip_at((place + 1) % chips, chips) * 2 + core
    before = chip_at((place + chips - 1) % chips, chips) * 2 + core
    twin = chip * 2 + 1 - core
    half = rows // 2
    mine = (left_ref, right_ref)
    gathered = (all_left, all_right)
    blocks = (block_left, block_right)

    barrier = pltpu.get_barrier_semaphore()
    for other in (after, before, twin):
        pl.semaphore_signal(barrier, inc=1, device_id={"blk": other}, device_id_type=MESH)
    pl.semaphore_wait(barrier, 3)

    def source(group, way):
        shift = (chips - group) if way == 0 else group
        return chip_at((place + shift) % chips, chips) * 2

    def ring_copy(group, way, part, src=None, arrived=0):
        ref = gathered[part].at[source(group + arrived, way) + core, pl.ds(way * half, half)]
        return pltpu.make_async_remote_copy(
            src_ref=ref if src is None else src,
            dst_ref=ref,
            send_sem=ring_send.at[group, way, part],
            recv_sem=ring_recv.at[group, way, part],
            device_id={"blk": after if way == 0 else before},
            device_id_type=MESH,
        )

    def twin_copy(group, way, part, src=None, side=core):
        ref = gathered[part].at[source(group, way) + side, pl.ds(way * half, half)]
        return pltpu.make_async_remote_copy(
            src_ref=ref if src is None else src,
            dst_ref=ref,
            send_sem=twin_send.at[group, way, part],
            recv_sem=twin_recv.at[group, way, part],
            device_id={"blk": twin},
            device_id_type=MESH,
        )

    own_copies = []
    for part in range(2):
        for way in range(2):
            piece = mine[part].at[pl.ds(way * half, half)]
            ring_copy(0, way, part, piece).start()
    for part in range(2):
        own_copies.append(
            pltpu.make_async_copy(mine[part], gathered[part].at[me], own_sem.at[part])
        )
        own_copies[-1].start()
        for way in range(2):
            piece = mine[part].at[pl.ds(way * half, half)]
            twin_copy(0, way, part, piece).start()
    own_copies.append(pltpu.make_async_copy(act_ref, act, own_sem.at[2]))
    own_copies[-1].start()
    own_copies.append(pltpu.make_async_copy(grad_ref, grad, own_sem.at[3]))
    own_copies[-1].start()
    for copy in own_copies:
        copy.wait()

    def step(group, carry):
        @pl.when(group < chips - 1)
        def _():
            for part in range(2):
                for way in range(2):
                    ring_copy(group, way, part, arrived=1).wait_recv()

                    @pl.when(group < chips - 2)
                    def _():
                        ring_copy(group + 1, way, part).start()

                    twin_copy(group + 1, way, part).start()

        loads = []
        for part in range(2):
            for way in range(2):
                twin_copy(group, way, part, side=1 - core).wait_recv()
                for side in range(2):
                    slot = way * 2 + side
                    load = pltpu.make_async_copy(
                        gathered[part].at[source(group, way) + side, pl.ds(way * half, half)],
                        blocks[part].at[pl.ds(slot * half, half)],
                        load_sem.at[slot, part],
                    )
                    load.start()
                    loads.append(load)
        for load in loads:
            load.wait()
        for part, (data, out) in enumerate(((act, proj_left), (grad, proj_right))):
            width = data.shape[1]
            tile = wide_tile(width)
            total[...] = jnp.zeros_like(total)

            @pl.loop(0, width // tile)
            def _(index):
                columns = pl.ds(pl.multiple_of(index * tile, tile), tile)
                total[...] += contract(blocks[part][:, columns], data[:, columns])

            for way in range(2):
                for side in range(2):
                    slot = way * 2 + side
                    start = (source(group, way) + side) * rows + way * half
                    out[pl.ds(pl.multiple_of(start, half), half), :] = total[
                        slot * half : (slot + 1) * half, :
                    ].astype(out.dtype)
        return carry

    lax.fori_loop(0, chips, step, 0)

    def drain(group, carry):
        for part in range(2):
            for way in range(2):
                @pl.when(group < chips - 1)
                def _():
                    ring_copy(group, way, part).wait_send()

                twin_copy(group, way, part).wait_send()
        return carry

    lax.fori_loop(0, chips, drain, 0)


def spread_kernel(chips, root, chunk, basis_ref, out_ref, own_sem, ring_send, ring_recv, twin_send, twin_recv):
    me = lax.axis_index("blk")
    chip, core = me // 2, me % 2
    place = place_of(chip, chips)
    after = chip_at((place + 1) % chips, chips) * 2 + core
    before = chip_at((place + chips - 1) % chips, chips) * 2 + core
    twin = chip * 2 + 1 - core
    hops = (place - place_of(root // 2, chips) + chips) % chips
    count = ring_send.shape[1]

    barrier = pltpu.get_barrier_semaphore()
    for other in (after, before, twin):
        pl.semaphore_signal(barrier, inc=1, device_id={"blk": other}, device_id_type=MESH)
    pl.semaphore_wait(barrier, 3)

    def rows_of(lane, way, index):
        start = ((lane * 2 + way) * count + index) * chunk
        return pl.ds(pl.multiple_of(start, chunk), chunk)

    def ring_copy(way, index, src=out_ref):
        rows = rows_of(core, way, index)
        return pltpu.make_async_remote_copy(
            src_ref=src.at[rows],
            dst_ref=out_ref.at[rows],
            send_sem=ring_send.at[way, index],
            recv_sem=ring_recv.at[way, index],
            device_id={"blk": after if way == 0 else before},
            device_id_type=MESH,
        )

    def twin_copy(lane, way, index, src=out_ref):
        rows = rows_of(lane, way, index)
        return pltpu.make_async_remote_copy(
            src_ref=src.at[rows],
            dst_ref=out_ref.at[rows],
            send_sem=twin_send.at[lane, way, index],
            recv_sem=twin_recv.at[lane, way, index],
            device_id={"blk": twin},
            device_id_type=MESH,
        )

    @pl.when(me == root)
    def _():
        own = pltpu.make_async_copy(basis_ref, out_ref, own_sem)

        @pl.loop(0, count)
        def _(index):
            for way in range(2):
                twin_copy(1 - core, way, index, basis_ref).start()
                ring_copy(way, index, basis_ref).start()

        own.start()

        @pl.loop(0, count)
        def _(index):
            for way in range(2):
                twin_copy(core, way, index, basis_ref).start()

        @pl.loop(0, count)
        def _(index):
            for way in range(2):
                twin_copy(1 - core, way, index, basis_ref).wait_send()
                ring_copy(way, index, basis_ref).wait_send()
                twin_copy(core, way, index, basis_ref).wait_send()

        own.wait()

    @pl.when((hops == 0) & (me != root))
    def _():
        @pl.loop(0, count)
        def _(index):
            for way in range(2):
                twin_copy(core, way, index).wait_recv()
                ring_copy(way, index).start()

        @pl.loop(0, count)
        def _(index):
            for way in range(2):
                twin_copy(1 - core, way, index).wait_recv()
                ring_copy(way, index).wait_send()

    @pl.when(hops > 0)
    def _():
        @pl.loop(0, count + chips)
        def _(tick):
            for way in range(2):
                gone = hops if way == 0 else chips - hops
                index = tick - gone

                @pl.when((index >= 0) & (index < count))
                def _():
                    ring_copy(way, index).wait_recv()

                    @pl.when(gone < chips - 1)
                    def _():
                        ring_copy(way, index).start()

                    twin_copy(core, way, index).start()

        @pl.loop(0, count)
        def _(index):
            for way in range(2):
                gone = hops if way == 0 else chips - hops
                twin_copy(1 - core, way, index).wait_recv()
                twin_copy(core, way, index).wait_send()

                @pl.when(gone < chips - 1)
                def _():
                    ring_copy(way, index).wait_send()


def spread(basis, size, root, first_id):
    quarter = basis.shape[0] // 4
    chunk = 128
    while quarter % chunk:
        chunk //= 2
    count = quarter // chunk
    return pl.pallas_call(
        functools.partial(spread_kernel, size // 2, root, chunk),
        out_shape=jax.ShapeDtypeStruct(basis.shape, basis.dtype),
        in_specs=[HBM],
        out_specs=HBM,
        scratch_shapes=[
            pltpu.SemaphoreType.DMA,
            pltpu.SemaphoreType.DMA((2, count)),
            pltpu.SemaphoreType.DMA((2, count)),
            pltpu.SemaphoreType.DMA((2, 2, count)),
            pltpu.SemaphoreType.DMA((2, 2, count)),
        ],
        compiler_params=pltpu.CompilerParams(
            collective_id=first_id + root, has_side_effects=True, vmem_limit_bytes=60 * 1024 * 1024
        ),
        cost_estimate=pl.CostEstimate(flops=0, bytes_accessed=2 * basis.size, transcendentals=0),
    )(basis)


def from_owner(basis, size, owner, first_id):
    branches = [
        functools.partial(spread, size=size, root=root, first_id=first_id) for root in range(size)
    ]
    return lax.switch(owner, branches, basis)


def gather_project(activations, output_grads, left, right, size):
    chips = size // 2
    rows = left.shape[0]
    slots = activations.shape[0]
    widths = (left.shape[1], right.shape[1])
    out = jax.ShapeDtypeStruct((size * rows, slots), jnp.bfloat16)
    vmem = pl.BlockSpec(memory_space=pltpu.VMEM)
    flops = 2 * size * rows * slots * sum(widths)
    return pl.pallas_call(
        functools.partial(gather_kernel, chips, rows),
        out_shape=[
            out,
            out,
            jax.ShapeDtypeStruct((size, rows, widths[0]), jnp.bfloat16),
            jax.ShapeDtypeStruct((size, rows, widths[1]), jnp.bfloat16),
        ],
        in_specs=[HBM] * 4,
        out_specs=[vmem, vmem, HBM, HBM],
        scratch_shapes=[
            pltpu.VMEM(activations.shape, jnp.bfloat16),
            pltpu.VMEM(output_grads.shape, jnp.bfloat16),
            pltpu.VMEM((2 * rows, widths[0]), jnp.bfloat16),
            pltpu.VMEM((2 * rows, widths[1]), jnp.bfloat16),
            pltpu.VMEM((2 * rows, slots), jnp.float32),
            pltpu.SemaphoreType.DMA((4, 2)),
            pltpu.SemaphoreType.DMA((4,)),
            pltpu.SemaphoreType.DMA((chips - 1, 2, 2)),
            pltpu.SemaphoreType.DMA((chips - 1, 2, 2)),
            pltpu.SemaphoreType.DMA((chips, 2, 2)),
            pltpu.SemaphoreType.DMA((chips, 2, 2)),
        ],
        compiler_params=pltpu.CompilerParams(
            collective_id=0, has_side_effects=True, vmem_limit_bytes=48 * 1024 * 1024
        ),
        cost_estimate=pl.CostEstimate(
            flops=flops, bytes_accessed=4 * size * rows * sum(widths), transcendentals=0
        ),
    )(activations, output_grads, left, right)[:2]


def make_local(mesh):
    size = mesh.shape["blk"]

    def local(
        activations,
        output_grads,
        query_left,
        query_right,
        basis_inputs,
        eigen_inputs,
        basis_outputs,
        eigen_outputs,
        owners,
        seq_lengths,
    ):
        basis_left, eigen_left = (
            from_owner(basis_inputs[0], size, owners[0], 1),
            broadcast(eigen_inputs[0], "blk", owners[0]),
        )
        basis_right, eigen_right = (
            from_owner(basis_outputs[0], size, owners[1], 1 + size),
            broadcast(eigen_outputs[0], "blk", owners[1]),
        )
        query_rank = query_left.shape[1]
        left_flat = query_left.reshape(-1, query_left.shape[2])
        right_flat = query_right.reshape(-1, query_right.shape[2])
        left_coeffs = jnp.dot(left_flat, basis_left, preferred_element_type=jnp.float32)
        right_coeffs = jnp.dot(right_flat, basis_right, preferred_element_type=jnp.float32)
        split = left_coeffs.shape[1]
        coeffs = jnp.concatenate([left_coeffs, right_coeffs], axis=1).astype(jnp.bfloat16)
        coeffs = lax.psum(coeffs, "grp").astype(jnp.float32)
        left_ready = finish(left_flat, coeffs[:, :split], basis_left, eigen_left)
        right_ready = finish(right_flat, coeffs[:, split:], basis_right, eigen_right)
        new_left, new_right = gather_project(
            activations, output_grads, left_ready, right_ready, size
        )
        slot_count = activations.shape[0]
        member = membership(seq_lengths, slot_count)
        both = jnp.stack([new_left, new_right])
        share = lax.psum_scatter(both, "grp", scatter_dimension=2, tiled=True)
        share = share.astype(jnp.float32)
        width = share.shape[2]
        product = (share[0] * share[1]).reshape(-1, query_rank, width)
        token_scores = jnp.sum(product, axis=1)
        member_part = lax.dynamic_slice_in_dim(
            member, lax.axis_index("grp") * width, width, 1
        )
        partial_scores = lax.dot_general(
            member_part,
            token_scores,
            (((1,), (1,)), ((), ())),
            precision=lax.Precision.HIGHEST,
            preferred_element_type=jnp.float32,
        )
        return lax.psum(partial_scores, "grp")

    return local


def solution(mesh):
    in_specs = (
        P("blk", "grp"),
        P("blk", "grp"),
        P("blk", None, "grp"),
        P("blk", None, "grp"),
        P("blk", "grp", None),
        P("blk", None),
        P("blk", "grp", None),
        P("blk", None),
        P(),
        P("blk"),
    )
    return jax.shard_map(
        make_local(mesh), mesh=mesh, in_specs=in_specs, out_specs=P("blk", None), check_vma=False
    )
```

time: 651 us -> 811 us (1.25)
  Pallas kernels: 0 us -> 696 us
  waiting for transfers between devices: 516 us -> 32.5 us
  matrix products: 59.1 us -> 21.3 us
    pallas_call x0 -> x3, Pallas kernels: none -> 696 us  [the longest x2 499 us: spread(): pl.pallas_call(functools.partial(spread_kernel, size // 2, root, chunk),...]
    psum x2 -> x1, waiting for transfers between devices: 290 us -> 0.02 us  [local(): coeffs = lax.psum(coeffs, 'grp').astype(jnp.float32)]
    all_gather x2 -> x0, waiting for transfers between devices: 203 us -> none  [the longest x1 138 us: local(): lax.all_gather(right_ready, 'blk', axis=0, tiled=True)]
    dot_general x4 -> x2, matrix products: 46.1 us -> 11.1 us  [contract(): lax.dot_general(row_block, factors, (((1,), (1,)), ((), ())), preferred_e...]
    reduce_scatter x2 -> x1, waiting for transfers between devices: 22 us -> 32.4 us  [local(): share = lax.psum_scatter(both, 'grp', scatter_dimension=2, tiled=True)]
    psum x2 -> x1, blocking collectives: 14.3 us -> 5.51 us  [local(): return lax.psum(partial_scores, 'grp')]
  transfers between devices with their start and end apart: 6 -> 2, of which waited for: 5 -> 1; matrix products, arithmetic and copies ran while one was open for 7% -> 0% of each run, Pallas kernels for 0% -> 0%
where the time goes in v1:
time: 811 us; the launch traced here: 817 us
  Pallas kernels  696 us (86%)
  blocking collectives  43.7 us (5%)
  waiting for transfers between devices  32.5 us (4%)
  matrix products  21.3 us (3%)
  between operations  16.2 us (2%)
    pallas_call x2, Pallas kernels, spread(): pl.pallas_call(functools.partial(spread_kernel, size // 2, root, chunk),...  499 us
    pallas_call x1, Pallas kernels, gather_project(): pl.pallas_call(functools.partial(gather_kernel, chips, rows), out_shape=[...  197 us
    psum x1, blocking collectives, broadcast(): return lax.psum(jnp.where(mine, x, jnp.zeros_like(x)), axis)  38.2 us
    reduce_scatter x1, waiting for transfers between devices, local(): share = lax.psum_scatter(both, 'grp', scatter_dimension=2, tiled=True)  32.4 us
  transfers between devices with their start and end apart: 2, of which 1 were waited for; matrix products, arithmetic and copies ran while one was open for 0% of the time, Pallas kernels for 0%

profile of v1, /device:TPU:0, one launch (start us, length us, event | category | flops | bytes accessed | tf_op | source)
XLA Modules:
  0.0 816.9 jit_solution(5831531297382736439)
XLA Ops:
  6.5 1.3 fusion.21
  9.2 158.6 %conditional.3 = (bf16[14336,512]{1,0:T(8,128)(2,1)}) conditional(s32[]{:T(128)} %clamp.7, bf16[14336,512]{1,0:T(8,128)(2,1)} %bitcast.25, bf16[14336,512]{1,0:T(8,128)(2,1)} %bitcast.26, bf16[14336,512]{1,0:T(8,128)(2,1)} %bitcast.27, bf16[14336,512]{1,0:T(8,128)(2,1)} %bitcast.28, ...), branch_computations={%region_17.18_spmd, %region_18.19_spmd, %region_19.20_spmd, %regio... | conditional | bytes 14680072 | solution.py:361
  9.2 158.3 %branch_6_fun.3 = bf16[14336,512]{1,0:T(8,128)(2,1)} custom-call(bf16[14336,512]{1,0:T(8,128)(2,1)} %basis_ref.22), custom_call_target="tpu_custom_call" | custom-call | bytes 14680064 | tf_op jit(solution)/shard_map/cond/branch_6_fun/pallas_call | solution.py:338
  167.7 8.0 fusion.2
  175.7 340.7 %conditional.2 = (bf16[4096,256]{1,0:T(8,128)(2,1)}) conditional(s32[]{:T(128)} %clamp.6, bf16[4096,256]{1,0:T(8,128)(2,1)S(1)} %bitcast.41, bf16[4096,256]{1,0:T(8,128)(2,1)S(1)} %bitcast.42, bf16[4096,256]{1,0:T(8,128)(2,1)S(1)} %bitcast.43, bf16[4096,256]{1,0:T(8,128)(2,1)S(1)} %bitcast.44, ...), branch_computations={%region_1.0_spmd, %region_2.0_spmd, %region_3.0_spmd, %region_4.0_... | conditional | bytes 2097160 | solution.py:361
  175.8 340.6 %branch_11_fun.2 = bf16[4096,256]{1,0:T(8,128)(2,1)} custom-call(bf16[4096,256]{1,0:T(8,128)(2,1)S(1)} %basis_ref.11), custom_call_target="tpu_custom_call" | custom-call | bytes 2097152 | tf_op jit(solution)/shard_map/cond/branch_11_fun/pallas_call | solution.py:338
  516.5 2.1 fusion.3
  518.5 0.7 pad_maximum_fusion.1
  519.2 0.0 reduce-scatter.2.cloned.1.call-start
  520.6 38.2 %all-reduce = (bf16[256]{0:T(256)(128)(2,1)S(1)}, bf16[512]{0:T(512)(128)(2,1)S(1)}) all-reduce(bf16[256]{0:T(256)(128)(2,1)S(1)} %fusion.20, bf16[512]{0:T(512)(128)(2,1)S(1)} %fusion.16), channel_id=1, replica_groups=mesh['blk'=16,'grp'=2] {'blk'}, use_global_device_ids=true, to_apply=%region_34.35 | all-reduce | flops 768 | bytes 3072 | tf_op jit(solution)/shard_map/psum | solution.py:16
  558.9 0.0 all-reduce.3.cloned.1.call-done
  558.9 0.9 convert_element_type.33
  559.8 10.3 %fusion.right_ref = bf16[64,14336]{1,0:T(8,128)(2,1)S(1)} fusion(bf16[14336,512]{1,0:T(8,128)(2,1)} %get-tuple-element.80, bf16[64,14336]{1,0:T(8,128)(2,1)} %bitcast.57, f32[64,768]{1,0:T(8,128)S(1)} %convert_element_type.33, f32[512]{0:T(512)S(1)} %add_divide_fusion), kind=kOutput, calls=%fused_computation.1 | convolution fusion | flops 942342144 | bytes 18483200 | tf_op jit(solution)/shard_map/dot_general | solution.py:20
  570.2 0.8 fusion.1.left_ref
  570.9 197.0 %shard_map.100 = (bf16[1024,512]{1,0:T(8,128)(2,1)S(1)}, bf16[1024,512]{1,0:T(8,128)(2,1)S(1)}, bf16[16,64,4096]{2,1,0:T(8,128)(2,1)}, bf16[16,64,14336]{2,1,0:T(8,128)(2,1)}) custom-call(bf16[512,4096]{1,0:T(8,128)(2,1)} %act_ref.1, bf16[512,14336]{1,0:T(8,128)(2,1)} %grad_ref.1, bf16[64,4096]{1,0:T(8,128)(2,1)S(1)} %fusion.1.left_ref, ...), custom_call_target="tpu_custom_call" | custom-call | flops 19327352832 | bytes 75497472 | tf_op jit(solution)/shard_map/pallas_call | solution.py:372
  767.9 1.5 pad_maximum_fusion
  769.4 0.6 copy-done.6
  770.1 0.2 reduce-window.8
  770.2 32.4 %reduce-scatter.2.cloned.1.call-done = bf16[2,1024,256]{2,1,0:T(8,128)(2,1)} async-done(((bf16[2,1024,512]{2,1,0:T(8,128)(2,1)}), bf16[2,1024,256]{2,1,0:T(8,128)(2,1)}) %reduce-scatter.2.cloned.1.call-update) | async-done | bytes 1048592 | tf_op jit(solution)/shard_map/reduce_scatter | solution.py:443
  802.7 1.4 convert_element_type.41
  804.1 0.1 slice_multiply_fusion
  804.2 0.1 reduce_sum.9
  804.3 0.2 fusion.13
  804.5 5.5 psum.31
  (21 shorter events, 0.1 us)
Async XLA Ops:
  6.5 552.4 %all-reduce.3.cloned.1.call-start = ((), (), s32[]{:S(2)}) async-start(), calls=%async_computation.1 | async-start | bytes 196608 | tf_op jit(solution)/shard_map/psum | solution.py:434
  9.1 158.6 %copy-start.2 = (bf16[2,32,14336]{2,1,0:T(8,128)(2,1)S(1)}, bf16[2,32,14336]{2,1,0:T(8,128)(2,1)}, u32[]{:S(2)}) copy-start(bf16[2,32,14336]{2,1,0:T(8,128)(2,1)} %param.45) | copy-start | bytes 5505028
  167.7 8.0 copy-start
  175.7 340.7 %copy-start.3 = (bf16[2,32,4096]{2,1,0:T(8,128)(2,1)S(1)}, bf16[2,32,4096]{2,1,0:T(8,128)(2,1)}, u32[]{:S(2)}) copy-start(bf16[2,32,4096]{2,1,0:T(8,128)(2,1)} %param.44) | copy-start | bytes 1572868
  516.4 4.1 copy-start.4
  516.4 4.1 copy-start.5
  519.2 283.5 %reduce-scatter.2.cloned.1.call-start = ((), (), s32[]{:S(2)}) async-start(), calls=%async_computation.2 | async-start | bytes 3145728 | tf_op jit(solution)/shard_map/reduce_scatter | solution.py:443
  559.8 10.3 %copy-start.1 = (bf16[4096,256]{1,0:T(8,128)(2,1)S(1)}, bf16[4096,256]{1,0:T(8,128)(2,1)}, u32[]{:S(2)}) copy-start(bf16[4096,256]{1,0:T(8,128)(2,1)} %get-tuple-element.79) | copy-start | bytes 6291460
  769.4 0.7 copy-start.6
Sparse Core Ops, SparseCore 0:
  519.3 26.2 all-reduce.2
  769.6 33.0 reduce-scatter.1

commit v2 on v1

--- a/solution.py
+++ b/solution.py
@@ -9,11 +9,6 @@
 
 MESH = pl.DeviceIdType.MESH
 HBM = pl.BlockSpec(memory_space=pltpu.HBM)
-
-
-def broadcast(x, axis, root):
-    mine = lax.axis_index(axis) == root
-    return lax.psum(jnp.where(mine, x, jnp.zeros_like(x)), axis)
 
 
 def contract(row_block, factors):
@@ -142,8 +137,12 @@
             piece = mine[part].at[pl.ds(way * half, half)]
             ring_copy(0, way, part, piece).start()
     for part in range(2):
+        own_rows = blocks[part].at[pl.ds(0, rows)]
+        fetch = pltpu.make_async_copy(mine[part], own_rows, own_sem.at[part])
+        fetch.start()
+        fetch.wait()
         own_copies.append(
-            pltpu.make_async_copy(mine[part], gathered[part].at[me], own_sem.at[part])
+            pltpu.make_async_copy(own_rows, gathered[part].at[me], own_sem.at[part])
         )
         own_copies[-1].start()
         for way in range(2):
@@ -218,7 +217,7 @@
     lax.fori_loop(0, chips, drain, 0)
 
 
-def spread_kernel(chips, root, chunk, basis_ref, out_ref, own_sem, ring_send, ring_recv, twin_send, twin_recv):
+def spread_kernel(chips, root, chunk, basis_ref, out_ref, stage, own_sem, ring_send, ring_recv, twin_send, twin_recv):
     me = lax.axis_index("blk")
     chip, core = me // 2, me % 2
     place = place_of(chip, chips)
@@ -261,15 +260,17 @@
 
     @pl.when(me == root)
     def _():
-        own = pltpu.make_async_copy(basis_ref, out_ref, own_sem)
-
         @pl.loop(0, count)
         def _(index):
             for way in range(2):
                 twin_copy(1 - core, way, index, basis_ref).start()
                 ring_copy(way, index, basis_ref).start()
 
-        own.start()
+        fetch = pltpu.make_async_copy(basis_ref, stage, own_sem.at[0])
+        fetch.start()
+        fetch.wait()
+        store = pltpu.make_async_copy(stage, out_ref, own_sem.at[1])
+        store.start()
 
         @pl.loop(0, count)
         def _(index):
@@ -283,7 +284,7 @@
                 ring_copy(way, index, basis_ref).wait_send()
                 twin_copy(core, way, index, basis_ref).wait_send()
 
-        own.wait()
+        store.wait()
 
     @pl.when((hops == 0) & (me != root))
     def _():
@@ -301,11 +302,11 @@
 
     @pl.when(hops > 0)
     def _():
-        @pl.loop(0, count + chips)
+        @pl.loop(0, count + 2 * chips)
         def _(tick):
             for way in range(2):
                 gone = hops if way == 0 else chips - hops
-                index = tick - gone
+                index = tick - 2 * gone
 
                 @pl.when((index >= 0) & (index < count))
                 def _():
@@ -341,7 +342,8 @@
         in_specs=[HBM],
         out_specs=HBM,
         scratch_shapes=[
-            pltpu.SemaphoreType.DMA,
+            pltpu.VMEM(basis.shape, basis.dtype),
+            pltpu.SemaphoreType.DMA((2,)),
             pltpu.SemaphoreType.DMA((2, count)),
             pltpu.SemaphoreType.DMA((2, count)),
             pltpu.SemaphoreType.DMA((2, 2, count)),
@@ -359,6 +361,21 @@
         functools.partial(spread, size=size, root=root, first_id=first_id) for root in range(size)
     ]
     return lax.switch(owner, branches, basis)
+
+
+def exchange_sum(value, axis, count, width):
+    me = lax.axis_index(axis)
+
+    def part(index):
+        if width is None:
+            return value
+        return lax.dynamic_slice_in_dim(value, index * width, width, value.ndim - 1)
+
+    total = part(me).astype(jnp.float32)
+    for shift in range(1, count):
+        pairs = [(index, (index + shift) % count) for index in range(count)]
+        total += lax.ppermute(part((me + shift) % count), axis, pairs).astype(jnp.float32)
+    return total
 
 
 def gather_project(activations, output_grads, left, right, size):
@@ -403,6 +420,7 @@
 
 def make_local(mesh):
     size = mesh.shape["blk"]
+    groups = mesh.shape["grp"]
 
     def local(
         activations,
@@ -416,22 +434,20 @@
         owners,
         seq_lengths,
     ):
-        basis_left, eigen_left = (
-            from_owner(basis_inputs[0], size, owners[0], 1),
-            broadcast(eigen_inputs[0], "blk", owners[0]),
-        )
-        basis_right, eigen_right = (
-            from_owner(basis_outputs[0], size, owners[1], 1 + size),
-            broadcast(eigen_outputs[0], "blk", owners[1]),
-        )
+        eigens = jnp.concatenate([eigen_inputs, eigen_outputs], axis=1)
+        eigens = lax.all_gather(eigens, "blk", axis=0, tiled=True)
+        split = eigen_inputs.shape[1]
+        eigen_left = lax.dynamic_index_in_dim(eigens[:, :split], owners[0], 0, keepdims=False)
+        eigen_right = lax.dynamic_index_in_dim(eigens[:, split:], owners[1], 0, keepdims=False)
+        basis_left = from_owner(basis_inputs[0], size, owners[0], 1)
+        basis_right = from_owner(basis_outputs[0], size, owners[1], 1 + size)
         query_rank = query_left.shape[1]
         left_flat = query_left.reshape(-1, query_left.shape[2])
         right_flat = query_right.reshape(-1, query_right.shape[2])
         left_coeffs = jnp.dot(left_flat, basis_left, preferred_element_type=jnp.float32)
         right_coeffs = jnp.dot(right_flat, basis_right, preferred_element_type=jnp.float32)
-        split = left_coeffs.shape[1]
         coeffs = jnp.concatenate([left_coeffs, right_coeffs], axis=1).astype(jnp.bfloat16)
-        coeffs = lax.psum(coeffs, "grp").astype(jnp.float32)
+        coeffs = exchange_sum(coeffs, "grp", groups, None)
         left_ready = finish(left_flat, coeffs[:, :split], basis_left, eigen_left)
         right_ready = finish(right_flat, coeffs[:, split:], basis_right, eigen_right)
         new_left, new_right = gather_project(
@@ -440,9 +456,8 @@
         slot_count = activations.shape[0]
         member = membership(seq_lengths, slot_count)
         both = jnp.stack([new_left, new_right])
-        share = lax.psum_scatter(both, "grp", scatter_dimension=2, tiled=True)
-        share = share.astype(jnp.float32)
-        width = share.shape[2]
+        width = slot_count // groups
+        share = exchange_sum(both, "grp", groups, width)
         product = (share[0] * share[1]).reshape(-1, query_rank, width)
         token_scores = jnp.sum(product, axis=1)
         member_part = lax.dynamic_slice_in_dim(

time: 811 us -> 446 us (0.55)
  Pallas kernels: 696 us -> 354 us
  blocking collectives: 43.7 us -> 32 us
  between operations: 16.2 us -> 5.57 us
  waiting for transfers between devices: 32.5 us -> 24.3 us
    pallas_call x2, Pallas kernels: 499 us -> 153 us  [spread(): pl.pallas_call(functools.partial(spread_kernel, size // 2, root, chunk),...]
    psum x1 -> x0, blocking collectives: 38.2 us -> none  [broadcast(): return lax.psum(jnp.where(mine, x, jnp.zeros_like(x)), axis)]
    reduce_scatter x1 -> x0, waiting for transfers between devices: 32.4 us -> none  [local(): share = lax.psum_scatter(both, 'grp', scatter_dimension=2, tiled=True)]
    all_gather x0 -> x1, blocking collectives: none -> 26.5 us  [local(): eigens = lax.all_gather(eigens, 'blk', axis=0, tiled=True)]
    ppermute x0 -> x2, waiting for transfers between devices: none -> 24.3 us  [exchange_sum(): lax.ppermute(part((me + shift) % count), axis, pairs).astype(jnp.float32)]
where the time goes in v2:
time: 446 us
  Pallas kernels  354 us (79%)
  blocking collectives  32 us (7%)
  waiting for transfers between devices  24.3 us (5%)
  matrix products  22.2 us (5%)
  between operations  5.57 us (1%)
    pallas_call x1, Pallas kernels, gather_project(): pl.pallas_call(functools.partial(gather_kernel, chips, rows), out_shape=[...  201 us
    pallas_call x2, Pallas kernels, spread(): pl.pallas_call(functools.partial(spread_kernel, size // 2, root, chunk),...  153 us
    all_gather x1, blocking collectives, local(): eigens = lax.all_gather(eigens, 'blk', axis=0, tiled=True)  26.5 us
    ppermute x2, waiting for transfers between devices, exchange_sum(): lax.ppermute(part((me + shift) % count), axis, pairs).astype(jnp.float32)  24.3 us
    dot_general x2, matrix products, contract(): lax.dot_general(row_block, factors, (((1,), (1,)), ((), ())), preferred_e...  11.8 us
  transfers between devices with their start and end apart: 2, of which 1 were waited for; matrix products, arithmetic and copies ran while one was open for 0% of the time, Pallas kernels for 0%

profile of v2, /device:TPU:0, one launch (start us, length us, event | category | flops | bytes accessed | tf_op | source)
XLA Modules:
  0.0 446.0 jit_solution(6920501068087939489)
XLA Ops:
  0.0 1.3 fusion.22
  2.7 0.0 copy-start.3
  2.7 107.0 %conditional.3 = (bf16[14336,512]{1,0:T(8,128)(2,1)}) conditional(s32[]{:T(128)} %clamp.7, bf16[14336,512]{1,0:T(8,128)(2,1)} %bitcast.34, bf16[14336,512]{1,0:T(8,128)(2,1)} %bitcast.35, bf16[14336,512]{1,0:T(8,128)(2,1)} %bitcast.36, bf16[14336,512]{1,0:T(8,128)(2,1)} %bitcast.37, ...), branch_computations={%region_17.18_spmd, %region_18.19_spmd, %region_19.20_spmd, %regio... | conditional | bytes 14680072 | solution.py:363
  2.9 106.5 %branch_14_fun.3 = bf16[14336,512]{1,0:T(8,128)(2,1)} custom-call(bf16[14336,512]{1,0:T(8,128)(2,1)} %basis_ref.30), custom_call_target="tpu_custom_call" | custom-call | bytes 14680064 | tf_op jit(solution)/shard_map/cond/branch_14_fun/pallas_call | solution.py:339
  109.7 8.0 %fusion.2 = bf16[64,512]{1,0:T(8,128)(2,1)S(1)} fusion(bf16[64,14336]{1,0:T(8,128)(2,1)S(1)} %bitcast.66, bf16[14336,512]{1,0:T(8,128)(2,1)} %get-tuple-element.78), kind=kOutput, calls=%fused_computation.10 | convolution fusion | flops 939556864 | bytes 16580608 | tf_op jit(solution)/shard_map/dot_general | solution.py:448
  117.7 46.6 %conditional.2 = (bf16[4096,256]{1,0:T(8,128)(2,1)}) conditional(s32[]{:T(128)} %clamp.6, bf16[4096,256]{1,0:T(8,128)(2,1)S(1)} %bitcast.50, bf16[4096,256]{1,0:T(8,128)(2,1)S(1)} %bitcast.51, bf16[4096,256]{1,0:T(8,128)(2,1)S(1)} %bitcast.52, bf16[4096,256]{1,0:T(8,128)(2,1)S(1)} %bitcast.53, ...), branch_computations={%region_1.2_spmd, %region_2.3_spmd, %region_3.4_spmd, %region_4.5_... | conditional | bytes 2097160 | solution.py:363
  117.7 46.5 %branch_14_fun.2 = bf16[4096,256]{1,0:T(8,128)(2,1)} custom-call(bf16[4096,256]{1,0:T(8,128)(2,1)S(1)} %basis_ref.14), custom_call_target="tpu_custom_call" | custom-call | bytes 2097152 | tf_op jit(solution)/shard_map/cond/branch_14_fun/pallas_call | solution.py:339
  164.2 0.0 copy-start.5
  164.3 2.2 fusion.3
  166.5 1.6 collective-permute-start
  170.8 26.5 %all-gather = bf16[16,1,768]{2,1,0:T(2,128)(2,1)S(1)} all-gather(bf16[1,1,768]{2,1,0:T(2,128)(2,1)S(1)} %maximum_bitcast_fusion), channel_id=1, replica_groups=mesh['blk'=16,'grp'=2] {'blk'}, dimensions={0}, use_global_device_ids=true | all-gather | bytes 26112 | tf_op jit(solution)/shard_map/all_gather | solution.py:438
  198.8 11.1 %fusion.right_ref = bf16[64,14336]{1,0:T(8,128)(2,1)} fusion(bf16[14336,512]{1,0:T(8,128)(2,1)} %get-tuple-element.78, bf16[64,14336]{1,0:T(8,128)(2,1)S(1)} %bitcast.67, f32[64,768]{1,0:T(8,128)S(1)} %convert_add_fusion.1, f32[512]{0:T(512)S(1)} %bitcast.73), kind=kOutput, calls=%fused_computation.1 | convolution fusion | flops 942342144 | bytes 18483200 | tf_op jit(solution)/shard_map/dot_general | solution.py:15
  209.9 0.8 fusion.1.left_ref
  210.7 0.7 copy-done
  211.4 201.1 %shard_map.100 = (bf16[1024,512]{1,0:T(8,128)(2,1)S(1)}, bf16[1024,512]{1,0:T(8,128)(2,1)S(1)}, bf16[16,64,4096]{2,1,0:T(8,128)(2,1)}, bf16[16,64,14336]{2,1,0:T(8,128)(2,1)}) custom-call(bf16[512,4096]{1,0:T(8,128)(2,1)} %act_ref.1, bf16[512,14336]{1,0:T(8,128)(2,1)} %grad_ref.1, bf16[64,4096]{1,0:T(8,128)(2,1)S(1)} %fusion.1.left_ref, ...), custom_call_target="tpu_custom_call" | custom-call | flops 19327352832 | bytes 75497472 | tf_op jit(solution)/shard_map/pallas_call | solution.py:389
  412.6 1.1 fusion.4
  413.6 0.5 collective-permute-start.1
  414.1 0.2 reduce-window.8
  414.3 24.3 %collective-permute-done.1 = bf16[2,1024,256]{2,1,0:T(8,128)(2,1)} collective-permute-done((bf16[2,1024,256]{2,1,0:T(8,128)(2,1)}, bf16[2,1024,256]{2,1,0:T(8,128)(2,1)}, u32[]{:S(2)}, u32[]{:S(2)}) %collective-permute-start.1) | collective-permute-done | bytes 1048608 | tf_op jit(solution)/shard_map/ppermute | solution.py:377
  438.6 1.4 convert_add_fusion
  440.1 0.1 slice_multiply_fusion
  440.2 0.1 reduce_sum.9
  440.3 0.2 fusion.15
  440.5 5.5 %psum.7 = f32[4,32]{1,0:T(4,128)} all-reduce(f32[4,32]{1,0:T(4,128)S(1)} %fusion.15), channel_id=1, replica_groups=mesh['blk'=16,'grp'=2] {'grp'}, use_global_device_ids=true, to_apply=%region_34.35 | all-reduce | flops 128 | bytes 1024 | tf_op jit(solution)/shard_map/psum | solution.py:473
  (23 shorter events, 0.1 us)
Async XLA Ops:
  2.7 107.0 %copy-start.3 = (bf16[2,32,14336]{2,1,0:T(8,128)(2,1)S(1)}, bf16[2,32,14336]{2,1,0:T(8,128)(2,1)}, u32[]{:S(2)}) copy-start(bf16[2,32,14336]{2,1,0:T(8,128)(2,1)} %param.45) | copy-start | bytes 5505028
  109.7 8.0 %copy-start.1 = (bf16[1,4096,256]{2,1,0:T(8,128)(2,1)S(1)}, bf16[1,4096,256]{2,1,0:T(8,128)(2,1)}, u32[]{:S(2)}) copy-start(bf16[1,4096,256]{2,1,0:T(8,128)(2,1)} %param.46) | copy-start | bytes 6291460
  164.2 6.5 %copy-start.5 = (bf16[1,512]{1,0:T(2,128)(2,1)S(1)}, bf16[1,512]{1,0:T(2,128)(2,1)}, u32[]{:S(2)}) copy-start(bf16[1,512]{1,0:T(2,128)(2,1)} %param.49) | copy-start | bytes 3076
  164.3 6.5 %copy-start.6 = (bf16[1,256]{1,0:T(2,128)(2,1)S(1)}, bf16[1,256]{1,0:T(2,128)(2,1)}, u32[]{:S(2)}) copy-start(bf16[1,256]{1,0:T(2,128)(2,1)} %param.47) | copy-start | bytes 1540
  166.5 32.2 %collective-permute-start = (bf16[64,768]{1,0:T(8,128)(2,1)S(1)}, bf16[64,768]{1,0:T(8,128)(2,1)S(1)}, u32[]{:S(2)}, u32[]{:S(2)}) collective-permute-start(bf16[64,768]{1,0:T(8,128)(2,1)S(1)} %pad_maximum_fusion), channel_id=1, source_target_pairs={{0,1},{1,0},{2,3},{3,2},{4,5},{5,4},{6,7},{7,6},{8,9},{9,8},{10,11... | collective-permute-start | bytes 294920 | tf_op jit(solution)/shard_map/ppermute | solution.py:377
  198.8 11.1 %copy-start.2 = (bf16[4096,256]{1,0:T(8,128)(2,1)S(1)}, bf16[4096,256]{1,0:T(8,128)(2,1)}, u32[]{:S(2)}) copy-start(bf16[4096,256]{1,0:T(8,128)(2,1)} %get-tuple-element.77) | copy-start | bytes 6291460
  198.8 11.1 %copy-start.4 = (bf16[2,32,4096]{2,1,0:T(8,128)(2,1)S(1)}, bf16[2,32,4096]{2,1,0:T(8,128)(2,1)}, u32[]{:S(2)}) copy-start(bf16[2,32,4096]{2,1,0:T(8,128)(2,1)} %param.44) | copy-start | bytes 1572868
  209.9 1.5 copy-start
  412.5 1.6 copy-start.7
  413.6 25.0 %collective-permute-start.1 = (bf16[2,1024,256]{2,1,0:T(8,128)(2,1)}, bf16[2,1024,256]{2,1,0:T(8,128)(2,1)}, u32[]{:S(2)}, u32[]{:S(2)}) collective-permute-start(bf16[2,1024,256]{2,1,0:T(8,128)(2,1)} %fusion.4), channel_id=1, source_target_pairs={{0,1},{1,0},{2,3},{3,2},{4,5},{5,4},{6,7},{7,6},{8,9},{9,8},{10,11... | collective-permute-start | bytes 3145736 | tf_op jit(solution)/shard_map/ppermute | solution.py:377
